TPU v7x, 512 devices: a whole 4x8x8 slice. The times are simulated.
512 devices in a mesh: dx: 8 (over z), dy: 8 (over y_hi, x), dz: 8 (over y_lo, core).
Axes of the slice: x: 4, y: 8 (y_hi: 2, y_lo: 4; y = y_hi * 4 + y_lo), z: 8, core: 2. Of those that a mesh axis runs over, the one named last changes fastest.
Arguments:
- node_state: bfloat16 [16, 16, 16, 32, 128], P('dx', 'dy', 'dz'), may hold values from -6 to 6
- mesh_base: int32 [3, 16, 16, 16, 32], P(None, 'dx', 'dy', 'dz'), may hold values from 0 to 255, as said below
- mesh_frac: float32 [3, 16, 16, 16, 32], P(None, 'dx', 'dy', 'dz'), may hold values from 0 to 1
- charge: float32 [16, 16, 16, 32], P('dx', 'dy', 'dz'), may hold values from -0.5 to 0.5
- nbr_code: int32 [16, 16, 16, 32, 128], P('dx', 'dy', 'dz'), may hold values from 0 to 863, as said below
- nbr_count: int32 [16, 16, 16, 32], P('dx', 'dy', 'dz'), may hold values from 32 to 128, as said below
- radial_weight: float32 [8, 128], replicated, may hold values from -2 to 2
- mix_weight: bfloat16 [3, 128, 128], replicated, may hold values from -0.5 to 0.5
- force_weight: float32 [128], replicated, may hold values from -0.5 to 0.5
Outputs:
- node_next: bfloat16 [16, 16, 16, 32, 128], P('dx', 'dy', 'dz')
- forces: float32 [3, 16, 16, 16, 32], P(None, 'dx', 'dy', 'dz')
Inputs may be any that keep to these rules, and one draw needn't show every extreme that they name: `mesh_base`: entry d of an atom in octant (X, Y, Z) lies in the atom's octant: from 32 / 2 times its octant index along d up to 16 more, exclusive. In every octant the first atom sits at the lower end and the second at the upper end in every dimension. `nbr_code`: The first atom of every octant has the largest code in its first slot and 0 in its second. `nbr_count`: slots from the count on are padding. The first atom of every octant has 128 live slots, the second 128 // 4.
All inputs are finite; a program needn't handle non-finite values.
Results may differ from a plain program's by a relative error of at most 0.00095.
The roundings to bfloat16 on the way count: a program that leaves them out, or rounds other values in their place, can miss the bound.
Values may be sent and summed in bfloat16 or wider, within the bound.
A program may use at most 64 MiB of HBM per device.

v0:
```python
import math
import jax
import jax.numpy as jnp
from jax import lax
from jax.sharding import PartitionSpec as P

NB = 8
NBR = 128
MB = 32
KZW = 8
cell_size = 1.13
ewald_beta = 0.625
coulomb = 332.0637
sigma_low = 8.0
sigma_rate = 1.5
highest = lax.Precision.HIGHEST


def with_halo(cells, sides, width):
    for axis, dim in sides:
        count = lax.axis_size(axis)
        head = lax.slice_in_dim(cells, 0, width, axis=dim)
        tail = lax.slice_in_dim(cells, cells.shape[dim] - width, cells.shape[dim], axis=dim)
        cells = jnp.concatenate(
            [
                lax.ppermute(tail, axis, [(i, (i + 1) % count) for i in range(count)]),
                cells,
                lax.ppermute(head, axis, [((i + 1) % count, i) for i in range(count)]),
            ],
            axis=dim,
        )
    return cells


def spline_terms(fraction):
    remainder = 1.0 - fraction
    frac_square = fraction * fraction
    frac_cube = frac_square * fraction
    weights = jnp.stack(
        [
            remainder * remainder * remainder / 6.0,
            (3.0 * frac_cube - 6.0 * frac_square + 4.0) / 6.0,
            (-3.0 * frac_cube + 3.0 * frac_square + 3.0 * fraction + 1.0) / 6.0,
            frac_cube / 6.0,
        ]
    )
    slopes = jnp.stack(
        [
            -0.5 * remainder * remainder,
            1.5 * frac_square - 2.0 * fraction,
            -1.5 * frac_square + fraction + 0.5,
            0.5 * frac_square,
        ]
    )
    return (weights, slopes)


def harmonics(direction):
    unit_x, unit_y, unit_z = (direction[0], direction[1], direction[2])
    root_three = math.sqrt(3.0)
    root_fifteen = math.sqrt(15.0)
    root_five = math.sqrt(5.0)
    return jnp.stack(
        [
            jnp.ones_like(unit_x),
            root_three * unit_x,
            root_three * unit_y,
            root_three * unit_z,
            root_fifteen * unit_x * unit_y,
            root_fifteen * unit_y * unit_z,
            0.5 * root_five * (3.0 * unit_z * unit_z - 1.0),
            root_fifteen * unit_x * unit_z,
            0.5 * root_fifteen * (unit_x * unit_x - unit_y * unit_y),
        ]
    )


def edge_terms(displace, active):
    square = jnp.sum(displace * displace, axis=0)
    direction = displace / jnp.sqrt(square + 1.0)
    angular = harmonics(direction)
    distance = cell_size * jnp.sqrt(square)
    widths = sigma_low * jnp.power(sigma_rate, jnp.arange(NB).astype(jnp.float32))
    radial = jnp.exp(-jnp.square(distance[None] / widths[:, None, None]))
    products = radial[:, None] * angular[None] * active.astype(jnp.float32)[None, None]
    atom_rows = displace.shape[1]
    return jnp.transpose(products, (2, 0, 1, 3)).reshape(atom_rows, NB * 9, -1).astype(jnp.bfloat16)


def node_update(edge_values, neighbour_state, own_state, radial_weight, mix_weight, force_weight):
    summed = jnp.einsum(
        "bkn,bnc->bkc", edge_values, neighbour_state, preferred_element_type=jnp.float32
    )
    atom_rows = summed.shape[0]
    summed = summed.reshape(atom_rows, NB, 9, -1)
    message = (jnp.sum(summed * radial_weight[None, :, None, :], axis=1) / math.sqrt(NBR)).astype(
        jnp.bfloat16
    )
    scalar = jnp.dot(message[:, 0], mix_weight[0], preferred_element_type=jnp.float32)
    vector = jnp.einsum(
        "bmc,cd->bmd", message[:, 1:4], mix_weight[1], preferred_element_type=jnp.float32
    )
    tensor = jnp.einsum(
        "bmc,cd->bmd", message[:, 4:9], mix_weight[2], preferred_element_type=jnp.float32
    )
    invariant = scalar + jnp.sum(tensor * tensor, axis=1)
    gating = jax.nn.sigmoid(invariant)
    updated = (own_state.astype(jnp.float32) + jax.nn.silu(invariant)).astype(jnp.bfloat16)
    short_push = jnp.sum(vector * (gating * force_weight)[:, None, :], axis=2)
    return (updated, jnp.transpose(short_push))


def phases(wavenumber, cell_index, extent):
    return 2.0 * math.pi / extent * jnp.mod(wavenumber * cell_index, extent).astype(jnp.float32)


def cell_table(coeff, local_cells, cell_index):
    table = jnp.zeros((local_cells.shape[0], cell_index.shape[0]), jnp.float32)
    for stencil in range(4):
        match = (cell_index[None, :] == (local_cells + stencil)[:, None]).astype(jnp.float32)
        table = table + coeff[stencil][:, None] * match
    return table


def influence(modes_x, modes_y, modes_z, length_x, length_y, length_z):

    def folded(wavenumber, extent):
        return jnp.where(2 * wavenumber >= extent, wavenumber - extent, wavenumber).astype(
            jnp.float32
        ) / (cell_size * extent)

    wave_square = (
        jnp.square(folded(modes_x, length_x))
        + jnp.square(folded(modes_y, length_y))
        + jnp.square(folded(modes_z, length_z))
    )
    volume = cell_size**3 * length_x * length_y * length_z
    return (
        coulomb
        / (math.pi * volume)
        * jnp.exp(-math.pi**2 * wave_square / ewald_beta**2)
        / wave_square
    )


def shards(
    node_state,
    mesh_base,
    mesh_frac,
    charge,
    nbr_code,
    nbr_count,
    radial_weight,
    mix_weight,
    force_weight,
):
    count_x = lax.axis_size("dx")
    count_y = lax.axis_size("dy")
    count_z = lax.axis_size("dz")
    index_x = lax.axis_index("dx")
    index_y = lax.axis_index("dy")
    index_z = lax.axis_index("dz")
    octants = node_state.shape[3]
    channels = node_state.shape[4]
    atom_total = 8 * octants
    half_block = MB // 2
    block_cells = MB + 3
    length_x = MB * count_x
    length_y = MB * count_y
    length_z = MB * count_z
    places = mesh_base.astype(jnp.float32) + mesh_frac
    halo_state = with_halo(node_state, (("dx", 0), ("dy", 1), ("dz", 2)), 1)
    halo_places = with_halo(places, (("dx", 1), ("dy", 2), ("dz", 3)), 1)
    flat_state = halo_state.reshape(64 * octants, channels)
    flat_places = halo_places.reshape(3, 64 * octants)
    piece_rows = octants // 2
    slot_index = jnp.arange(NBR, dtype=jnp.int32)

    def one_block(inputs):
        block_id, code_rows, count_rows, own_places, state_rows = inputs
        octant = block_id // 2
        corner_x = octant // 4
        corner_y = octant // 2 % 2
        corner_z = octant % 2
        side_code = code_rows // octants
        slot_code = code_rows % octants
        step_x = side_code // 9 - 1
        step_y = side_code // 3 % 3 - 1
        step_z = side_code % 3 - 1
        neighbour = (
            ((corner_x + 1 + step_x) * 4 + corner_y + 1 + step_y) * 4 + corner_z + 1 + step_z
        ) * octants + slot_code
        reach_x = 2 * index_x + corner_x + step_x
        reach_y = 2 * index_y + corner_y + step_y
        reach_z = 2 * index_z + corner_z + step_z
        wrap_shift = jnp.stack(
            [
                (reach_x - jnp.mod(reach_x, 2 * count_x)) * half_block,
                (reach_y - jnp.mod(reach_y, 2 * count_y)) * half_block,
                (reach_z - jnp.mod(reach_z, 2 * count_z)) * half_block,
            ]
        ).astype(jnp.float32)
        displace = flat_places[:, neighbour] + wrap_shift - own_places[:, :, None]
        active = slot_index[None, :] < count_rows[:, None]
        edge_values = edge_terms(displace, active)
        return node_update(
            edge_values, flat_state[neighbour], state_rows, radial_weight, mix_weight, force_weight
        )

    updated, short_push = lax.map(
        one_block,
        (
            jnp.arange(16, dtype=jnp.int32),
            nbr_code.reshape(16, piece_rows, NBR),
            nbr_count.reshape(16, piece_rows),
            jnp.transpose(places.reshape(3, 16, piece_rows), (1, 0, 2)),
            node_state.reshape(16, piece_rows, channels),
        ),
    )
    node_next = updated.reshape(node_state.shape)
    short_force = jnp.transpose(short_push, (1, 0, 2)).reshape(3, atom_total)
    base_rows = mesh_base.reshape(3, atom_total)
    frac_rows = mesh_frac.reshape(3, atom_total)
    charge_rows = charge.reshape(atom_total)
    anchor_x = index_x * MB
    anchor_y = index_y * MB
    anchor_z = index_z * MB
    cell_index = jnp.arange(block_cells, dtype=jnp.int32)
    planes = 1 + jnp.arange(KZW, dtype=jnp.int32)
    rows_dev = MB * KZW // count_z
    row_start = (index_y * count_z + index_z) * rows_dev
    modes_x = jnp.arange(length_x, dtype=jnp.int32)
    weights, slopes = spline_terms(frac_rows)
    table_x = cell_table(weights[:, 0], base_rows[0] - anchor_x, cell_index)
    table_y = cell_table(weights[:, 1], base_rows[1] - anchor_y, cell_index)
    table_z = cell_table(weights[:, 2], base_rows[2] - anchor_z, cell_index)
    angle_z = phases(planes[None, :], (anchor_z + cell_index)[:, None], length_z)
    wave_z_re = jnp.dot(table_z, jnp.cos(angle_z), precision=highest)
    wave_z_im = -jnp.dot(table_z, jnp.sin(angle_z), precision=highest)

    def spread_part(inputs):
        part_x, part_y, part_re, part_im, part_charge = inputs
        left_side = jnp.transpose(part_x * part_charge[:, None])
        right_side = jnp.concatenate(
            [part_y[:, :, None] * part_re[:, None, :], part_y[:, :, None] * part_im[:, None, :]],
            axis=2,
        )
        return jnp.dot(left_side, right_side.reshape(part_x.shape[0], -1), precision=highest)

    spread = jnp.sum(
        lax.map(
            spread_part,
            (
                table_x.reshape(8, octants, block_cells),
                table_y.reshape(8, octants, block_cells),
                wave_z_re.reshape(8, octants, KZW),
                wave_z_im.reshape(8, octants, KZW),
                charge_rows.reshape(8, octants),
            ),
        ),
        axis=0,
    )
    spread = spread.reshape(block_cells, block_cells, 2, KZW)
    spread_re = spread[:, :, 0]
    spread_im = spread[:, :, 1]
    wave_count = lax.axis_size(("dy", "dz")) * rows_dev // KZW
    modes_y = jnp.arange(wave_count, dtype=jnp.int32)
    angle_y = phases(modes_y[None, :], (anchor_y + cell_index)[:, None], length_y)
    cos_y = jnp.cos(angle_y)
    sin_y = jnp.sin(angle_y)
    term_re = jnp.einsum("yk,xyz->kzx", cos_y, spread_re, precision=highest) + jnp.einsum(
        "yk,xyz->kzx", sin_y, spread_im, precision=highest
    )
    term_im = jnp.einsum("yk,xyz->kzx", cos_y, spread_im, precision=highest) - jnp.einsum(
        "yk,xyz->kzx", sin_y, spread_re, precision=highest
    )
    slab_rows = lax.psum_scatter(
        jnp.stack([term_re, term_im], axis=2).reshape(
            lax.axis_size(("dy", "dz")) * rows_dev, 2, block_cells
        ),
        ("dy", "dz"),
        scatter_dimension=0,
        tiled=True,
    )
    received = lax.all_gather(slab_rows[None], "dx", axis=0, tiled=True)
    shard_count = received.shape[0]
    cells_now = (jnp.arange(shard_count, dtype=jnp.int32) * MB)[:, None] + cell_index[None, :]
    angle_x = phases(cells_now.reshape(-1)[:, None], modes_x[None, :], length_x)
    cos_x = jnp.cos(angle_x)
    sin_x = jnp.sin(angle_x)
    lined_up = jnp.transpose(received, (1, 2, 0, 3)).reshape(received.shape[1], 2, -1)
    spec_re = jnp.dot(lined_up[:, 0], cos_x, precision=highest) + jnp.dot(
        lined_up[:, 1], sin_x, precision=highest
    )
    spec_im = jnp.dot(lined_up[:, 1], cos_x, precision=highest) - jnp.dot(
        lined_up[:, 0], sin_x, precision=highest
    )
    spectrum = jnp.stack([spec_re, spec_im], axis=1)
    global_rows = row_start + jnp.arange(rows_dev, dtype=jnp.int32)
    green_table = influence(
        modes_x[None, :],
        (global_rows // KZW)[:, None],
        (global_rows % KZW + 1)[:, None],
        length_x,
        length_y,
        length_z,
    )
    scaled = spectrum * green_table[:, None, :]
    angle_back = phases(modes_x[:, None], (anchor_x + cell_index)[None, :], length_x)
    cos_back = jnp.cos(angle_back)
    sin_back = jnp.sin(angle_back)
    back_re = jnp.dot(scaled[:, 0], cos_back, precision=highest) - jnp.dot(
        scaled[:, 1], sin_back, precision=highest
    )
    back_im = jnp.dot(scaled[:, 0], sin_back, precision=highest) + jnp.dot(
        scaled[:, 1], cos_back, precision=highest
    )
    back_rows = jnp.stack([back_re, back_im], axis=1)
    received = lax.all_gather(back_rows, ("dy", "dz"), axis=0, tiled=True)
    wave_count = received.shape[0] // KZW
    modes_y = jnp.arange(wave_count, dtype=jnp.int32)
    angle_y = phases(modes_y[:, None], (anchor_y + cell_index)[None, :], length_y)
    cos_y = jnp.cos(angle_y)
    sin_y = jnp.sin(angle_y)
    lined_up = received.reshape(wave_count, KZW, 2, block_cells)
    part_re = lined_up[:, :, 0]
    part_im = lined_up[:, :, 1]
    wave_re = jnp.einsum("kzx,ky->zxy", part_re, cos_y, precision=highest) - jnp.einsum(
        "kzx,ky->zxy", part_im, sin_y, precision=highest
    )
    wave_im = jnp.einsum("kzx,ky->zxy", part_re, sin_y, precision=highest) + jnp.einsum(
        "kzx,ky->zxy", part_im, cos_y, precision=highest
    )
    wave_rows = jnp.stack([wave_re, wave_im], axis=1)
    angle_z = phases(planes[:, None], (anchor_z + cell_index)[None, :], length_z)
    potential = 2.0 * (
        jnp.einsum("zxy,zw->xyw", wave_rows[:, 0], jnp.cos(angle_z), precision=highest)
        - jnp.einsum("zxy,zw->xyw", wave_rows[:, 1], jnp.sin(angle_z), precision=highest)
    )
    flat_potential = potential.reshape(block_cells, -1)
    slope_x = cell_table(slopes[:, 0], base_rows[0] - anchor_x, cell_index)
    slope_y = cell_table(slopes[:, 1], base_rows[1] - anchor_y, cell_index)
    slope_z = cell_table(slopes[:, 2], base_rows[2] - anchor_z, cell_index)

    def pull_force(inputs):
        part_x, part_slope_x, part_y, part_slope_y, part_z, part_slope_z = inputs
        values = jnp.dot(part_x, flat_potential, precision=highest).reshape(
            -1, block_cells, block_cells
        )
        tilted = jnp.dot(part_slope_x, flat_potential, precision=highest).reshape(
            -1, block_cells, block_cells
        )
        along_z = jnp.sum(values * part_z[:, None, :], axis=2)
        grad_x = jnp.sum(jnp.sum(tilted * part_z[:, None, :], axis=2) * part_y, axis=1)
        grad_y = jnp.sum(along_z * part_slope_y, axis=1)
        grad_z = jnp.sum(jnp.sum(values * part_slope_z[:, None, :], axis=2) * part_y, axis=1)
        return jnp.stack([grad_x, grad_y, grad_z])

    gradients = lax.map(
        pull_force,
        (
            table_x.reshape(8, octants, block_cells),
            slope_x.reshape(8, octants, block_cells),
            table_y.reshape(8, octants, block_cells),
            slope_y.reshape(8, octants, block_cells),
            table_z.reshape(8, octants, block_cells),
            slope_z.reshape(8, octants, block_cells),
        ),
    )
    long_force = -(charge_rows / cell_size) * jnp.transpose(gradients, (1, 0, 2)).reshape(
        3, atom_total
    )
    forces = (short_force + long_force).reshape(3, 2, 2, 2, octants)
    return (node_next, forces)


def solution(mesh):
    placed = (
        P("dx", "dy", "dz", None, None),
        P(None, "dx", "dy", "dz", None),
        P(None, "dx", "dy", "dz", None),
        P("dx", "dy", "dz", None),
        P("dx", "dy", "dz", None, None),
        P("dx", "dy", "dz", None),
        P(),
        P(),
        P(),
    )
    return jax.shard_map(
        shards,
        mesh=mesh,
        in_specs=placed,
        out_specs=(P("dx", "dy", "dz", None, None), P(None, "dx", "dy", "dz", None)),
        check_vma=False,
    )
```

profile of v0, /device:TPU:1, one launch (start us, length us, event | category | flops | bytes accessed | tf_op | source)
XLA Modules:
  0.0 621.4 jit_solution(17176939823443961220)
XLA Ops:
  12.7 5.2 while.36
  22.0 8.6 %copy.132 = f32[2048,2,35]{2,1,0:T(2,128)} copy(f32[2048,2,35]{2,0,1:T(8,128)S(1)} %pad_maximum_fusion.1) | data formatting | bytes 1146880 | tf_op jit(solution)/shard_map/stack | solution.py:278
  31.3 4.8 collective-permute-start
  36.1 8.6 %collective-permute-start.1 = (f32[3,1,2,2,32]{4,3,2,1,0:T(2,128)S(1)}, f32[3,1,2,2,32]{4,3,2,1,0:T(2,128)S(1)}, u32[]{:S(2)}, u32[]{:S(2)}) collective-permute-start(f32[3,1,2,2,32]{4,3,2,1,0:T(2,128)S(1)} %get-tuple-element.721), channel_id=1, source_target_pairs={{64,0},{128,64},{192,128},{256,192},{320,256},{384,320},{448,384},... | collective-permute-start | bytes 4616 | tf_op jit(solution)/shard_map/ppermute | solution.py:28
  46.7 4.6 collective-permute-start.7
  53.2 3.1 collective-permute-start.2
  56.3 8.4 %collective-permute-start.3 = (f32[3,4,1,2,32]{4,3,2,1,0:T(2,128)S(1)}, f32[3,4,1,2,32]{4,3,2,1,0:T(2,128)S(1)}, u32[]{:S(2)}, u32[]{:S(2)}) collective-permute-start(f32[3,4,1,2,32]{4,3,2,1,0:T(2,128)S(1)} %get-tuple-element.710), channel_id=1, source_target_pairs={{8,0},{16,8},{24,16},{32,24},{40,32},{48,40},{56,48},{0,56},{9,1},... | collective-permute-start | bytes 9224 | tf_op jit(solution)/shard_map/ppermute | solution.py:28
  67.6 9.8 %collective-permute-start.9 = (bf16[4,1,2,32,128]{4,3,2,1,0:T(8,128)(2,1)S(1)}, bf16[4,1,2,32,128]{4,3,2,1,0:T(8,128)(2,1)S(1)}, u32[]{:S(2)}, u32[]{:S(2)}) collective-permute-start(bf16[4,1,2,32,128]{4,3,2,1,0:T(8,128)(2,1)S(1)} %get-tuple-element.704), channel_id=1, source_target_pairs={{8,0},{16,8},{24,16},{32,24},{40,32},{48,40},{56,48},{0,56},{9,1},... | collective-permute-start | bytes 196616 | tf_op jit(solution)/shard_map/ppermute | solution.py:28
  77.5 6.0 collective-permute-start.4
  85.6 3.6 collective-permute-start.10
  89.2 2.6 collective-permute-start.11
  97.5 346.0 %while.38 = (s32[]{:T(128)}, bf16[16,16,128]{2,1,0:T(8,128)(2,1)}, f32[16,3,16]{2,1,0:T(4,128)}, bf16[16,16,128]{2,1,0:T(8,128)(2,1)S(1)}, s32[16]{0:T(128)S(1)}...) while((s32[]{:T(128)}, bf16[16,16,128]{2,1,0:T(8,128)(2,1)}, ...), condition=%wide.region_5.6_spmd.clone, body=%wide.region_0.5_spmd.clone.sunk | while | flops 43745308 | bytes 7252634 | solution.py:210
  101.8 5.5 gather_fusion.1
  110.3 6.2 gather_fusion
  123.4 5.5 gather_fusion.1
  132.0 6.2 gather_fusion
  145.0 5.5 gather_fusion.1
  153.6 6.2 gather_fusion
  166.6 5.5 gather_fusion.1
  175.2 6.2 gather_fusion
  188.3 5.5 gather_fusion.1
  196.8 6.2 gather_fusion
  209.9 5.5 gather_fusion.1
  218.4 6.2 gather_fusion
  231.5 5.5 gather_fusion.1
  240.1 6.2 gather_fusion
  253.1 5.5 gather_fusion.1
  261.7 6.2 gather_fusion
  274.8 5.5 gather_fusion.1
  283.3 6.2 gather_fusion
  296.4 5.5 gather_fusion.1
  304.9 6.2 gather_fusion
  318.0 5.5 gather_fusion.1
  326.6 6.2 gather_fusion
  339.6 5.5 gather_fusion.1
  348.2 6.2 gather_fusion
  361.2 5.5 gather_fusion.1
  369.8 6.2 gather_fusion
  382.8 5.5 gather_fusion.1
  391.4 6.2 gather_fusion
  404.5 5.5 gather_fusion.1
  413.0 6.2 gather_fusion
  426.1 5.5 gather_fusion.1
  434.6 6.2 gather_fusion
  445.1 18.5 %all-gather = f32[256,2,35]{2,1,0:T(2,128)S(1)} all-gather(f32[32,2,35]{2,1,0:T(2,128)S(1)} %constant_dynamic-slice_fusion.6), channel_id=2, replica_groups=mesh['dx'=8,'dy'=8,'dz'=8] {'dx'}, dimensions={0}, use_global_device_ids=true | all-gather | bytes 80640 | tf_op jit(solution)/shard_map/all_gather | solution.py:285
  463.9 2.1 fusion.115
  471.8 85.9 %all_gather.7 = f32[2048,2,35]{2,0,1:T(8,128)S(1)} all-gather(f32[32,2,35]{2,0,1:T(8,128)S(1)} %pad_maximum_fusion.6), channel_id=1, replica_groups=mesh['dx'=8,'dy'=8,'dz'=8] {'dy','dz'}, dimensions={0}, use_global_device_ids=true | all-gather | bytes 582400 | tf_op jit(solution)/shard_map/all_gather | solution.py:319
  564.3 49.6 %while.37 = (s32[]{:T(128)}, f32[8,3,32]{2,1,0:T(4,128)S(1)}, f32[8,32,35]{2,1,0:T(8,128)S(1)}, f32[35,1225]{1,0:T(8,128)S(1)}, f32[8,32,35]{2,1,0:T(8,128)S(1)}...) while((s32[]{:T(128)}, f32[8,3,32]{2,1,0:T(4,128)S(1)}, ...), condition=%wide.region_17.18_spmd, body=%wide.region_10.17_spmd.sunk | while | flops 33166656 | bytes 2277293 | solution.py:359
  565.0 2.7 multiply_reduce_fusion.7
  567.8 2.7 fusion.337
  571.2 2.7 multiply_reduce_fusion.7
  574.0 2.7 fusion.337
  577.4 2.7 multiply_reduce_fusion.7
  580.2 2.7 fusion.337
  583.6 2.7 multiply_reduce_fusion.7
  586.4 2.7 fusion.337
  589.8 2.7 multiply_reduce_fusion.7
  592.6 2.7 fusion.337
  596.0 2.7 multiply_reduce_fusion.7
  598.8 2.7 fusion.337
  602.2 2.7 multiply_reduce_fusion.7
  605.0 2.7 fusion.337
  608.4 2.7 multiply_reduce_fusion.7
  611.2 2.7 fusion.337
  (901 shorter events, 161.5 us)
Async XLA Ops:
  7.2 5.5 copy-start.9
  7.2 437.1 %all-reduce.3.cloned.1.call-start = ((), (), s32[]{:S(2)}) async-start(), calls=%async_computation | async-start | bytes 4194304
  7.2 3.2 copy-start.11
  8.1 2.5 copy-start.13
  30.5 14.2 %copy-start.1 = (bf16[2,2,2,32,128]{4,3,2,1,0:T(8,128)(2,1)S(1)}, bf16[2,2,2,32,128]{4,3,2,1,0:T(8,128)(2,1)}, u32[]{:S(2)}) copy-start(bf16[2,2,2,32,128]{4,3,2,1,0:T(8,128)(2,1)} %param.15) | copy-start | bytes 196612
  30.5 63.2 %copy-start.8 = (s32[2,2,2,32]{3,2,1,0:T(2,128)S(1)}, s32[2,2,2,32]{3,2,1,0:T(2,128)}, u32[]{:S(2)}) copy-start(s32[2,2,2,32]{3,2,1,0:T(2,128)} %param.20) | copy-start | bytes 3076
  31.3 21.8 %collective-permute-start = (f32[3,1,2,2,32]{4,3,2,1,0:T(2,128)S(1)}, f32[3,1,2,2,32]{4,3,2,1,0:T(2,128)S(1)}, u32[]{:S(2)}, u32[]{:S(2)}) collective-permute-start(f32[3,1,2,2,32]{4,3,2,1,0:T(2,128)S(1)} %get-tuple-element.720), channel_id=1, source_target_pairs={{0,64},{64,128},{128,192},{192,256},{256,320},{320,384},{384,448},... | collective-permute-start | bytes 4616 | tf_op jit(solution)/shard_map/ppermute | solution.py:26
  36.1 17.0 %collective-permute-start.1 = (f32[3,1,2,2,32]{4,3,2,1,0:T(2,128)S(1)}, f32[3,1,2,2,32]{4,3,2,1,0:T(2,128)S(1)}, u32[]{:S(2)}, u32[]{:S(2)}) collective-permute-start(f32[3,1,2,2,32]{4,3,2,1,0:T(2,128)S(1)} %get-tuple-element.721), channel_id=1, source_target_pairs={{64,0},{128,64},{192,128},{256,192},{320,256},{384,320},{448,384},... | collective-permute-start | bytes 4616 | tf_op jit(solution)/shard_map/ppermute | solution.py:28
  44.7 20.9 %collective-permute-start.6 = (bf16[1,2,2,32,128]{4,3,2,1,0:T(8,128)(2,1)S(1)}, bf16[1,2,2,32,128]{4,3,2,1,0:T(8,128)(2,1)S(1)}, u32[]{:S(2)}, u32[]{:S(2)}) collective-permute-start(bf16[1,2,2,32,128]{4,3,2,1,0:T(8,128)(2,1)S(1)} %get-tuple-element.706), channel_id=1, source_target_pairs={{0,64},{64,128},{128,192},{192,256},{256,320},{320,384},{384,448},... | collective-permute-start | bytes 98312 | tf_op jit(solution)/shard_map/ppermute | solution.py:26
  46.7 19.0 %collective-permute-start.7 = (bf16[1,2,2,32,128]{4,3,2,1,0:T(8,128)(2,1)S(1)}, bf16[1,2,2,32,128]{4,3,2,1,0:T(8,128)(2,1)S(1)}, u32[]{:S(2)}, u32[]{:S(2)}) collective-permute-start(bf16[1,2,2,32,128]{4,3,2,1,0:T(8,128)(2,1)S(1)} %get-tuple-element.705), channel_id=1, source_target_pairs={{64,0},{128,64},{192,128},{256,192},{320,256},{384,320},{448,384},... | collective-permute-start | bytes 98312 | tf_op jit(solution)/shard_map/ppermute | solution.py:28
  53.2 11.7 %collective-permute-start.2 = (f32[3,4,1,2,32]{4,3,2,1,0:T(2,128)S(1)}, f32[3,4,1,2,32]{4,3,2,1,0:T(2,128)S(1)}, u32[]{:S(2)}, u32[]{:S(2)}) collective-permute-start(f32[3,4,1,2,32]{4,3,2,1,0:T(2,128)S(1)} %get-tuple-element.709), channel_id=1, source_target_pairs={{0,8},{8,16},{16,24},{24,32},{32,40},{40,48},{48,56},{56,0},{1,9},... | collective-permute-start | bytes 9224 | tf_op jit(solution)/shard_map/ppermute | solution.py:26
  56.3 9.3 %collective-permute-start.3 = (f32[3,4,1,2,32]{4,3,2,1,0:T(2,128)S(1)}, f32[3,4,1,2,32]{4,3,2,1,0:T(2,128)S(1)}, u32[]{:S(2)}, u32[]{:S(2)}) collective-permute-start(f32[3,4,1,2,32]{4,3,2,1,0:T(2,128)S(1)} %get-tuple-element.710), channel_id=1, source_target_pairs={{8,0},{16,8},{24,16},{32,24},{40,32},{48,40},{56,48},{0,56},{9,1},... | collective-permute-start | bytes 9224 | tf_op jit(solution)/shard_map/ppermute | solution.py:28
  65.6 31.9 %copy-start.3 = (f32[8,128]{1,0:T(8,128)S(1)}, f32[8,128]{1,0:T(8,128)}, u32[]{:S(2)}) copy-start(f32[8,128]{1,0:T(8,128)} %param.21) | copy-start | bytes 12292
  65.6 31.9 %copy-start.7 = (f32[128]{0:T(128)S(1)}, f32[128]{0:T(128)}, u32[]{:S(2)}) copy-start(f32[128]{0:T(128)} %param.23) | copy-start | bytes 1540
  65.7 19.8 %collective-permute-start.8 = (bf16[4,1,2,32,128]{4,3,2,1,0:T(8,128)(2,1)S(1)}, bf16[4,1,2,32,128]{4,3,2,1,0:T(8,128)(2,1)S(1)}, u32[]{:S(2)}, u32[]{:S(2)}) collective-permute-start(bf16[4,1,2,32,128]{4,3,2,1,0:T(8,128)(2,1)S(1)} %get-tuple-element.703), channel_id=1, source_target_pairs={{0,8},{8,16},{16,24},{24,32},{32,40},{40,48},{48,56},{56,0},{1,9},... | collective-permute-start | bytes 196616 | tf_op jit(solution)/shard_map/ppermute | solution.py:26
  67.6 17.9 %collective-permute-start.9 = (bf16[4,1,2,32,128]{4,3,2,1,0:T(8,128)(2,1)S(1)}, bf16[4,1,2,32,128]{4,3,2,1,0:T(8,128)(2,1)S(1)}, u32[]{:S(2)}, u32[]{:S(2)}) collective-permute-start(bf16[4,1,2,32,128]{4,3,2,1,0:T(8,128)(2,1)S(1)} %get-tuple-element.704), channel_id=1, source_target_pairs={{8,0},{16,8},{24,16},{32,24},{40,32},{48,40},{56,48},{0,56},{9,1},... | collective-permute-start | bytes 196616 | tf_op jit(solution)/shard_map/ppermute | solution.py:28
  77.5 18.7 %collective-permute-start.4 = (f32[3,4,4,1,32]{4,3,2,1,0:T(1,128)S(1)}, f32[3,4,4,1,32]{4,3,2,1,0:T(1,128)S(1)}, u32[]{:S(2)}, u32[]{:S(2)}) collective-permute-start(f32[3,4,4,1,32]{4,3,2,1,0:T(1,128)S(1)} %get-tuple-element.707), channel_id=1, source_target_pairs={{0,1},{1,2},{2,3},{3,4},{4,5},{5,6},{6,7},{7,0},{8,9},{9,10},{10,1... | collective-permute-start | bytes 18440 | tf_op jit(solution)/shard_map/ppermute | solution.py:26
  83.6 12.7 %collective-permute-start.5 = (f32[3,4,4,1,32]{4,3,2,1,0:T(1,128)S(1)}, f32[3,4,4,1,32]{4,3,2,1,0:T(1,128)S(1)}, u32[]{:S(2)}, u32[]{:S(2)}) collective-permute-start(f32[3,4,4,1,32]{4,3,2,1,0:T(1,128)S(1)} %get-tuple-element.708), channel_id=1, source_target_pairs={{1,0},{2,1},{3,2},{4,3},{5,4},{6,5},{7,6},{0,7},{9,8},{10,9},{11,1... | collective-permute-start | bytes 18440 | tf_op jit(solution)/shard_map/ppermute | solution.py:28
  85.6 11.2 %collective-permute-start.10 = (bf16[4,4,1,32,128]{4,3,2,1,0:T(8,128)(2,1)S(1)}, bf16[4,4,1,32,128]{4,3,2,1,0:T(8,128)(2,1)S(1)}, u32[]{:S(2)}, u32[]{:S(2)}) collective-permute-start(bf16[4,4,1,32,128]{4,3,2,1,0:T(8,128)(2,1)S(1)} %get-tuple-element.701), channel_id=1, source_target_pairs={{0,1},{1,2},{2,3},{3,4},{4,5},{5,6},{6,7},{7,0},{8,9},{9,10},{10,1... | collective-permute-start | bytes 393224 | tf_op jit(solution)/shard_map/ppermute | solution.py:26
  89.2 8.1 %collective-permute-start.11 = (bf16[4,4,1,32,128]{4,3,2,1,0:T(8,128)(2,1)S(1)}, bf16[4,4,1,32,128]{4,3,2,1,0:T(8,128)(2,1)S(1)}, u32[]{:S(2)}, u32[]{:S(2)}) collective-permute-start(bf16[4,4,1,32,128]{4,3,2,1,0:T(8,128)(2,1)S(1)} %get-tuple-element.702), channel_id=1, source_target_pairs={{1,0},{2,1},{3,2},{4,3},{5,4},{6,5},{7,6},{0,7},{9,8},{10,9},{11,1... | collective-permute-start | bytes 393224 | tf_op jit(solution)/shard_map/ppermute | solution.py:28
  97.5 3.5 copy-start.15
  116.5 0.9 copy-start
  116.5 2.6 copy-start.16
  119.1 3.5 copy-start.15
  138.1 0.9 copy-start
  138.2 2.6 copy-start.16
  140.7 3.5 copy-start.15
  159.8 2.6 copy-start.16
  162.4 3.5 copy-start.15
  181.4 0.9 copy-start
  181.4 2.6 copy-start.16
  184.0 3.5 copy-start.15
  203.0 2.6 copy-start.16
  205.6 3.5 copy-start.15
  224.6 2.6 copy-start.16
  227.2 3.5 copy-start.15
  246.3 2.6 copy-start.16
  248.9 3.5 copy-start.15
  267.9 0.9 copy-start
  267.9 2.6 copy-start.16
  270.5 3.5 copy-start.15
  289.5 0.9 copy-start
  289.5 2.6 copy-start.16
  292.1 3.5 copy-start.15
  311.1 0.9 copy-start
  311.1 2.6 copy-start.16
  313.7 3.5 copy-start.15
  332.8 2.6 copy-start.16
  335.4 3.5 copy-start.15
  354.4 2.6 copy-start.16
  357.0 3.5 copy-start.15
  376.0 2.6 copy-start.16
  378.6 3.5 copy-start.15
  397.6 2.6 copy-start.16
  400.2 3.5 copy-start.15
  419.2 2.6 copy-start.16
  421.8 3.5 copy-start.15
  440.8 2.6 copy-start.16
  443.5 22.5 %copy-start.10 = (s32[280]{0:T(512)S(1)}, s32[280]{0:T(512)}, u32[]{:S(2)}) copy-start(s32[280]{0:T(512)} %add.995) | copy-start | bytes 3364
  465.9 4.2 copy-start.2
  466.0 4.2 copy-start.17
  558.2 3.0 copy-start.12
  558.3 3.0 copy-start.14
  560.6 3.7 copy-start.6
  (12 other events, 10.4 us)
Sparse Core Ops, SparseCore 0:
  30.7 205.6 all-reduce.2
where the time goes:
time: 626 us; the launch traced here: 621 us
  local copies, waits for them, and re-layouts  270 us (43%)
  blocking collectives  104 us (17%)
  matrix products  85.6 us (14%)
  starting transfers between devices  57.5 us (9%)
  loops' own time  48.7 us (8%)
  other arithmetic  38.5 us (6%)
  between operations  15.4 us (2%)
    gather x16, local copies, waits for them, and re-layouts, one_block(): flat_state[neighbour]  98.9 us
    gather x32, local copies, waits for them, and re-layouts, one_block(): displace = flat_places[:, neighbour] + wrap_shift - own_places[:, :, None]  92.9 us
    all_gather x1, blocking collectives, shards(): received = lax.all_gather(back_rows, ('dy', 'dz'), axis=0, tiled=True)  85.9 us
    another operation x1, loops' own time, shards(): lax.map(one_block, (jnp.arange(16, dtype=jnp.int32), nbr_code.reshape(16,...  47.9 us
    ppermute x6, starting transfers between devices, with_halo(): lax.ppermute(head, axis, [((i + 1) % count, i) for i in range(count)])  36 us
    dynamic_slice x48, local copies, waits for them, and re-layouts, shards(): lax.map(one_block, (jnp.arange(16, dtype=jnp.int32), nbr_code.reshape(16,...  22.2 us
    ppermute x6, starting transfers between devices, with_halo(): lax.ppermute(tail, axis, [(i, (i + 1) % count) for i in range(count)])  21.5 us
    dot_general x8, matrix products, pull_force(): jnp.dot(part_x, flat_potential, precision=highest)  21.3 us
  transfers between devices with their start and end apart: 13, of which 2 were waited for; matrix products, arithmetic and copies ran while one was open for 48% of the time, Pallas kernels for 0%

commit v1 on v0

--- a/solution.py
+++ b/solution.py
@@ -14,6 +14,11 @@
 sigma_low = 8.0
 sigma_rate = 1.5
 highest = lax.Precision.HIGHEST
+
+
+def gather_over(block, axis, along):
+    outgoing = jnp.stack([block] * lax.axis_size(axis))
+    return jnp.concatenate(lax.all_to_all(outgoing, axis, 0, 0), axis=along)
 
 
 def with_halo(cells, sides, width):
@@ -316,7 +321,7 @@
         scaled[:, 1], cos_back, precision=highest
     )
     back_rows = jnp.stack([back_re, back_im], axis=1)
-    received = lax.all_gather(back_rows, ("dy", "dz"), axis=0, tiled=True)
+    received = gather_over(back_rows, ("dy", "dz"), 0)
     wave_count = received.shape[0] // KZW
     modes_y = jnp.arange(wave_count, dtype=jnp.int32)
     angle_y = phases(modes_y[:, None], (anchor_y + cell_index)[None, :], length_y)

time: 626 us -> 712 us (1.14); the launches traced: 621 us -> 699 us
  waiting for transfers between devices: 1.35 us -> 141 us
  blocking collectives: 104 us -> 20.8 us
  starting transfers between devices: 57.5 us -> 74 us
  loops' own time: 48.7 us -> 40.4 us
    unnamed x2, waiting for transfers between devices: 0.03 us -> 139 us
    all_gather x1 -> x0, blocking collectives: 85.9 us -> none  [shards(): received = lax.all_gather(back_rows, ('dy', 'dz'), axis=0, tiled=True)]
    gather x32, local copies, waits for them, and re-layouts: 92.9 us -> 112 us  [one_block(): displace = flat_places[:, neighbour] + wrap_shift - own_places[:, :, None]]
    all_to_all x0 -> x1, starting transfers between devices: none -> 16.3 us  [gather_over(): return jnp.concatenate(lax.all_to_all(outgoing, axis, 0, 0), axis=along)]
    dynamic_slice x48, local copies, waits for them, and re-layouts: 22.2 us -> 9.44 us  [shards(): lax.map(one_block, (jnp.arange(16, dtype=jnp.int32), nbr_code.reshape(16,...]
    another operation x1, loops' own time: 47.9 us -> 39.3 us  [shards(): lax.map(one_block, (jnp.arange(16, dtype=jnp.int32), nbr_code.reshape(16,...]
  transfers between devices with their start and end apart: 13 -> 14, of which waited for: 2 -> 3; matrix products, arithmetic and copies ran while one was open for 48% -> 44% of each run, Pallas kernels for 0% -> 0%
where the time goes in v1:
time: 712 us; the launch traced here: 699 us
  local copies, waits for them, and re-layouts  277 us (39%)
  waiting for transfers between devices  141 us (20%)
  matrix products  90.6 us (13%)
  starting transfers between devices  74 us (10%)
  loops' own time  40.4 us (6%)
  other arithmetic  39.9 us (6%)
  blocking collectives  20.8 us (3%)
  between operations  15.7 us (2%)
    unnamed x2, waiting for transfers between devices  139 us
    gather x32, local copies, waits for them, and re-layouts, one_block(): displace = flat_places[:, neighbour] + wrap_shift - own_places[:, :, None]  112 us
    gather x16, local copies, waits for them, and re-layouts, one_block(): flat_state[neighbour]  98.9 us
    another operation x1, loops' own time, shards(): lax.map(one_block, (jnp.arange(16, dtype=jnp.int32), nbr_code.reshape(16,...  39.3 us
    ppermute x6, starting transfers between devices, with_halo(): lax.ppermute(head, axis, [((i + 1) % count, i) for i in range(count)])  36.2 us
    dot_general x8, matrix products, pull_force(): jnp.dot(part_slope_x, flat_potential, precision=highest)  26.9 us
    ppermute x6, starting transfers between devices, with_halo(): lax.ppermute(tail, axis, [(i, (i + 1) % count) for i in range(count)])  21.5 us
    dot_general x8, matrix products, pull_force(): jnp.dot(part_x, flat_potential, precision=highest)  21.3 us
  transfers between devices with their start and end apart: 14, of which 3 were waited for; matrix products, arithmetic and copies ran while one was open for 44% of the time, Pallas kernels for 0%

profile of v1, /device:TPU:1, one launch (start us, length us, event | category | flops | bytes accessed | tf_op | source)
XLA Modules:
  0.0 699.3 jit_solution(9795395722157677389)
XLA Ops:
  13.3 5.2 while.36
  22.6 8.6 %copy.134 = f32[2048,2,35]{2,1,0:T(2,128)} copy(f32[2048,2,35]{2,0,1:T(8,128)S(1)} %pad_maximum_fusion.1) | data formatting | bytes 1146880 | tf_op jit(solution)/shard_map/stack | solution.py:283
  31.9 4.8 collective-permute-start
  36.7 8.6 %collective-permute-start.1 = (f32[3,1,2,2,32]{4,3,2,1,0:T(2,128)S(1)}, f32[3,1,2,2,32]{4,3,2,1,0:T(2,128)S(1)}, u32[]{:S(2)}, u32[]{:S(2)}) collective-permute-start(f32[3,1,2,2,32]{4,3,2,1,0:T(2,128)S(1)} %get-tuple-element.721), channel_id=1, source_target_pairs={{64,0},{128,64},{192,128},{256,192},{320,256},{384,320},{448,384},... | collective-permute-start | bytes 4616 | tf_op jit(solution)/shard_map/ppermute | solution.py:33
  47.3 4.6 collective-permute-start.7
  53.2 3.1 collective-permute-start.2
  56.3 8.4 %collective-permute-start.3 = (f32[3,4,1,2,32]{4,3,2,1,0:T(2,128)S(1)}, f32[3,4,1,2,32]{4,3,2,1,0:T(2,128)S(1)}, u32[]{:S(2)}, u32[]{:S(2)}) collective-permute-start(f32[3,4,1,2,32]{4,3,2,1,0:T(2,128)S(1)} %get-tuple-element.710), channel_id=1, source_target_pairs={{8,0},{16,8},{24,16},{32,24},{40,32},{48,40},{56,48},{0,56},{9,1},... | collective-permute-start | bytes 9224 | tf_op jit(solution)/shard_map/ppermute | solution.py:33
  67.6 9.8 %collective-permute-start.9 = (bf16[4,1,2,32,128]{4,3,2,1,0:T(8,128)(2,1)S(1)}, bf16[4,1,2,32,128]{4,3,2,1,0:T(8,128)(2,1)S(1)}, u32[]{:S(2)}, u32[]{:S(2)}) collective-permute-start(bf16[4,1,2,32,128]{4,3,2,1,0:T(8,128)(2,1)S(1)} %get-tuple-element.704), channel_id=1, source_target_pairs={{8,0},{16,8},{24,16},{32,24},{40,32},{48,40},{56,48},{0,56},{9,1},... | collective-permute-start | bytes 196616 | tf_op jit(solution)/shard_map/ppermute | solution.py:33
  77.4 6.1 collective-permute-start.4
  85.5 3.6 collective-permute-start.10
  89.2 2.9 collective-permute-start.11
  97.4 139.0 %all-reduce.3.cloned.1.call-done = f32[2048,2,35]{2,1,0:T(2,128)} async-done(((f32[2048,2,35]{2,1,0:T(2,128)}), f32[2048,2,35]{2,1,0:T(2,128)}) %all-reduce.3.cloned.1.call-update) | async-done | bytes 573456
  237.1 20.8 %all-gather = f32[256,2,35]{2,1,0:T(2,128)S(1)} all-gather(f32[32,2,35]{2,1,0:T(2,128)S(1)} %constant_dynamic-slice_fusion.6), channel_id=2, replica_groups=mesh['dx'=8,'dy'=8,'dz'=8] {'dx'}, dimensions={0}, use_global_device_ids=true | all-gather | bytes 80640 | tf_op jit(solution)/shard_map/all_gather | solution.py:290
  265.7 3.4 reshape.1379
  269.1 16.3 %all-to-all-start = ((f32[64,1,2240]{2,1,0:T(1,128)}), f32[64,1,2240]{2,1,0:T(1,128)S(1)}, u32[]{:S(2)}, u32[]{:S(2)}) async-start(f32[64,1,2240]{2,1,0:T(1,128)} %reshape.1379), calls=%async_computation | async-start | bytes 1179648 | tf_op jit(solution)/shard_map/all_to_all | solution.py:21
  285.5 337.7 %while.38 = (s32[]{:T(128)}, bf16[16,16,128]{2,1,0:T(8,128)(2,1)}, f32[16,3,16]{2,1,0:T(4,128)}, bf16[16,16,128]{2,1,0:T(8,128)(2,1)S(1)}, s32[16]{0:T(128)S(1)}...) while((s32[]{:T(128)}, bf16[16,16,128]{2,1,0:T(8,128)(2,1)}, ...), condition=%wide.region_5.6_spmd.clone, body=%wide.region_0.5_spmd.clone.sunk | while | flops 43745308 | bytes 6858822 | solution.py:215
  289.2 6.7 gather_fusion.1
  298.2 6.2 gather_fusion
  310.3 6.7 gather_fusion.1
  319.3 6.2 gather_fusion
  331.4 6.7 gather_fusion.1
  340.4 6.2 gather_fusion
  352.5 6.7 gather_fusion.1
  361.5 6.2 gather_fusion
  373.6 6.7 gather_fusion.1
  382.6 6.2 gather_fusion
  394.6 6.7 gather_fusion.1
  403.7 6.2 gather_fusion
  415.8 6.7 gather_fusion.1
  424.8 6.2 gather_fusion
  436.9 6.7 gather_fusion.1
  445.9 6.2 gather_fusion
  458.0 6.7 gather_fusion.1
  467.0 6.2 gather_fusion
  479.1 6.7 gather_fusion.1
  488.2 6.2 gather_fusion
  500.2 6.7 gather_fusion.1
  509.3 6.2 gather_fusion
  521.3 6.7 gather_fusion.1
  530.4 6.2 gather_fusion
  542.4 6.7 gather_fusion.1
  551.5 6.2 gather_fusion
  563.5 6.7 gather_fusion.1
  572.6 6.2 gather_fusion
  584.6 6.7 gather_fusion.1
  593.7 6.2 gather_fusion
  605.7 6.7 gather_fusion.1
  614.8 6.2 gather_fusion
  626.6 2.7 reshape.1380
  636.1 55.5 %while.37 = (s32[]{:T(128)}, f32[8,3,32]{2,1,0:T(4,128)S(1)}, f32[8,32,35]{2,1,0:T(8,128)}, f32[35,1225]{1,0:T(8,128)S(1)}, f32[8,32,35]{2,1,0:T(8,128)S(1)}, /*...) while((s32[]{:T(128)}, f32[8,3,32]{2,1,0:T(4,128)S(1)}, ...), condition=%wide.region_17.18_spmd, body=%wide.region_10.17_spmd.sunk | while | flops 33166656 | bytes 1720597 | solution.py:364
  639.8 3.4 fusion.337
  643.9 2.7 multiply_reduce_fusion.7
  646.7 3.4 fusion.337
  650.8 2.7 multiply_reduce_fusion.7
  653.6 3.4 fusion.337
  657.7 2.7 multiply_reduce_fusion.7
  660.5 3.4 fusion.337
  664.6 2.7 multiply_reduce_fusion.7
  667.4 3.4 fusion.337
  671.6 2.7 multiply_reduce_fusion.7
  674.4 3.4 fusion.337
  678.5 2.7 multiply_reduce_fusion.7
  681.3 3.4 fusion.337
  688.2 3.4 fusion.337
  (806 shorter events, 151.8 us)
Async XLA Ops:
  7.2 6.1 copy-start.7
  7.2 229.2 %all-reduce.3.cloned.1.call-start = ((), (), s32[]{:S(2)}) async-start(), calls=%async_computation.1 | async-start | bytes 4194304
  7.2 3.2 copy-start.8
  8.1 2.7 copy-start.10
  31.1 0.7 copy-start.3
  31.1 0.7 copy-start.4
  31.1 14.2 %copy-start.1 = (bf16[2,2,2,32,128]{4,3,2,1,0:T(8,128)(2,1)S(1)}, bf16[2,2,2,32,128]{4,3,2,1,0:T(8,128)(2,1)}, u32[]{:S(2)}) copy-start(bf16[2,2,2,32,128]{4,3,2,1,0:T(8,128)(2,1)} %param.15) | copy-start | bytes 196612
  31.1 61.1 %copy-start.6 = (s32[2,2,2,32]{3,2,1,0:T(2,128)S(1)}, s32[2,2,2,32]{3,2,1,0:T(2,128)}, u32[]{:S(2)}) copy-start(s32[2,2,2,32]{3,2,1,0:T(2,128)} %param.20) | copy-start | bytes 3076
  31.9 21.2 %collective-permute-start = (f32[3,1,2,2,32]{4,3,2,1,0:T(2,128)S(1)}, f32[3,1,2,2,32]{4,3,2,1,0:T(2,128)S(1)}, u32[]{:S(2)}, u32[]{:S(2)}) collective-permute-start(f32[3,1,2,2,32]{4,3,2,1,0:T(2,128)S(1)} %get-tuple-element.720), channel_id=1, source_target_pairs={{0,64},{64,128},{128,192},{192,256},{256,320},{320,384},{384,448},... | collective-permute-start | bytes 4616 | tf_op jit(solution)/shard_map/ppermute | solution.py:31
  36.7 16.4 %collective-permute-start.1 = (f32[3,1,2,2,32]{4,3,2,1,0:T(2,128)S(1)}, f32[3,1,2,2,32]{4,3,2,1,0:T(2,128)S(1)}, u32[]{:S(2)}, u32[]{:S(2)}) collective-permute-start(f32[3,1,2,2,32]{4,3,2,1,0:T(2,128)S(1)} %get-tuple-element.721), channel_id=1, source_target_pairs={{64,0},{128,64},{192,128},{256,192},{320,256},{384,320},{448,384},... | collective-permute-start | bytes 4616 | tf_op jit(solution)/shard_map/ppermute | solution.py:33
  45.3 20.3 %collective-permute-start.6 = (bf16[1,2,2,32,128]{4,3,2,1,0:T(8,128)(2,1)S(1)}, bf16[1,2,2,32,128]{4,3,2,1,0:T(8,128)(2,1)S(1)}, u32[]{:S(2)}, u32[]{:S(2)}) collective-permute-start(bf16[1,2,2,32,128]{4,3,2,1,0:T(8,128)(2,1)S(1)} %get-tuple-element.706), channel_id=1, source_target_pairs={{0,64},{64,128},{128,192},{192,256},{256,320},{320,384},{384,448},... | collective-permute-start | bytes 98312 | tf_op jit(solution)/shard_map/ppermute | solution.py:31
  47.3 18.4 %collective-permute-start.7 = (bf16[1,2,2,32,128]{4,3,2,1,0:T(8,128)(2,1)S(1)}, bf16[1,2,2,32,128]{4,3,2,1,0:T(8,128)(2,1)S(1)}, u32[]{:S(2)}, u32[]{:S(2)}) collective-permute-start(bf16[1,2,2,32,128]{4,3,2,1,0:T(8,128)(2,1)S(1)} %get-tuple-element.705), channel_id=1, source_target_pairs={{64,0},{128,64},{192,128},{256,192},{320,256},{384,320},{448,384},... | collective-permute-start | bytes 98312 | tf_op jit(solution)/shard_map/ppermute | solution.py:33
  53.2 11.7 %collective-permute-start.2 = (f32[3,4,1,2,32]{4,3,2,1,0:T(2,128)S(1)}, f32[3,4,1,2,32]{4,3,2,1,0:T(2,128)S(1)}, u32[]{:S(2)}, u32[]{:S(2)}) collective-permute-start(f32[3,4,1,2,32]{4,3,2,1,0:T(2,128)S(1)} %get-tuple-element.709), channel_id=1, source_target_pairs={{0,8},{8,16},{16,24},{24,32},{32,40},{40,48},{48,56},{56,0},{1,9},... | collective-permute-start | bytes 9224 | tf_op jit(solution)/shard_map/ppermute | solution.py:31
  56.3 9.3 %collective-permute-start.3 = (f32[3,4,1,2,32]{4,3,2,1,0:T(2,128)S(1)}, f32[3,4,1,2,32]{4,3,2,1,0:T(2,128)S(1)}, u32[]{:S(2)}, u32[]{:S(2)}) collective-permute-start(f32[3,4,1,2,32]{4,3,2,1,0:T(2,128)S(1)} %get-tuple-element.710), channel_id=1, source_target_pairs={{8,0},{16,8},{24,16},{32,24},{40,32},{48,40},{56,48},{0,56},{9,1},... | collective-permute-start | bytes 9224 | tf_op jit(solution)/shard_map/ppermute | solution.py:33
  65.7 19.7 %collective-permute-start.8 = (bf16[4,1,2,32,128]{4,3,2,1,0:T(8,128)(2,1)S(1)}, bf16[4,1,2,32,128]{4,3,2,1,0:T(8,128)(2,1)S(1)}, u32[]{:S(2)}, u32[]{:S(2)}) collective-permute-start(bf16[4,1,2,32,128]{4,3,2,1,0:T(8,128)(2,1)S(1)} %get-tuple-element.703), channel_id=1, source_target_pairs={{0,8},{8,16},{16,24},{24,32},{32,40},{40,48},{48,56},{56,0},{1,9},... | collective-permute-start | bytes 196616 | tf_op jit(solution)/shard_map/ppermute | solution.py:31
  67.6 17.8 %collective-permute-start.9 = (bf16[4,1,2,32,128]{4,3,2,1,0:T(8,128)(2,1)S(1)}, bf16[4,1,2,32,128]{4,3,2,1,0:T(8,128)(2,1)S(1)}, u32[]{:S(2)}, u32[]{:S(2)}) collective-permute-start(bf16[4,1,2,32,128]{4,3,2,1,0:T(8,128)(2,1)S(1)} %get-tuple-element.704), channel_id=1, source_target_pairs={{8,0},{16,8},{24,16},{32,24},{40,32},{48,40},{56,48},{0,56},{9,1},... | collective-permute-start | bytes 196616 | tf_op jit(solution)/shard_map/ppermute | solution.py:33
  77.4 17.4 %collective-permute-start.4 = (f32[3,4,4,1,32]{4,3,2,1,0:T(1,128)S(1)}, f32[3,4,4,1,32]{4,3,2,1,0:T(1,128)S(1)}, u32[]{:S(2)}, u32[]{:S(2)}) collective-permute-start(f32[3,4,4,1,32]{4,3,2,1,0:T(1,128)S(1)} %get-tuple-element.707), channel_id=1, source_target_pairs={{0,1},{1,2},{2,3},{3,4},{4,5},{5,6},{6,7},{7,0},{8,9},{9,10},{10,1... | collective-permute-start | bytes 18440 | tf_op jit(solution)/shard_map/ppermute | solution.py:31
  83.5 11.4 %collective-permute-start.5 = (f32[3,4,4,1,32]{4,3,2,1,0:T(1,128)S(1)}, f32[3,4,4,1,32]{4,3,2,1,0:T(1,128)S(1)}, u32[]{:S(2)}, u32[]{:S(2)}) collective-permute-start(f32[3,4,4,1,32]{4,3,2,1,0:T(1,128)S(1)} %get-tuple-element.708), channel_id=1, source_target_pairs={{1,0},{2,1},{3,2},{4,3},{5,4},{6,5},{7,6},{0,7},{9,8},{10,9},{11,1... | collective-permute-start | bytes 18440 | tf_op jit(solution)/shard_map/ppermute | solution.py:33
  85.5 10.9 %collective-permute-start.10 = (bf16[4,4,1,32,128]{4,3,2,1,0:T(8,128)(2,1)S(1)}, bf16[4,4,1,32,128]{4,3,2,1,0:T(8,128)(2,1)S(1)}, u32[]{:S(2)}, u32[]{:S(2)}) collective-permute-start(bf16[4,4,1,32,128]{4,3,2,1,0:T(8,128)(2,1)S(1)} %get-tuple-element.701), channel_id=1, source_target_pairs={{0,1},{1,2},{2,3},{3,4},{4,5},{5,6},{6,7},{7,0},{8,9},{9,10},{10,1... | collective-permute-start | bytes 393224 | tf_op jit(solution)/shard_map/ppermute | solution.py:31
  89.2 8.2 %collective-permute-start.11 = (bf16[4,4,1,32,128]{4,3,2,1,0:T(8,128)(2,1)S(1)}, bf16[4,4,1,32,128]{4,3,2,1,0:T(8,128)(2,1)S(1)}, u32[]{:S(2)}, u32[]{:S(2)}) collective-permute-start(bf16[4,4,1,32,128]{4,3,2,1,0:T(8,128)(2,1)S(1)} %get-tuple-element.702), channel_id=1, source_target_pairs={{1,0},{2,1},{3,2},{4,3},{5,4},{6,5},{7,6},{0,7},{9,8},{10,9},{11,1... | collective-permute-start | bytes 393224 | tf_op jit(solution)/shard_map/ppermute | solution.py:33
  265.7 19.8 %copy-start = (bf16[3,128,128]{2,1,0:T(8,128)(2,1)S(1)}, bf16[3,128,128]{2,1,0:T(8,128)(2,1)}, u32[]{:S(2)}) copy-start(bf16[3,128,128]{2,1,0:T(8,128)(2,1)} %param.22) | copy-start | bytes 294916
  265.7 19.8 %copy-start.2 = (f32[8,128]{1,0:T(8,128)S(1)}, f32[8,128]{1,0:T(8,128)}, u32[]{:S(2)}) copy-start(f32[8,128]{1,0:T(8,128)} %param.21) | copy-start | bytes 12292
  265.7 19.8 %copy-start.5 = (f32[128]{0:T(128)S(1)}, f32[128]{0:T(128)}, u32[]{:S(2)}) copy-start(f32[128]{0:T(128)} %param.23) | copy-start | bytes 1540
  269.1 354.9 %all-to-all-start = ((f32[64,1,2240]{2,1,0:T(1,128)}), f32[64,1,2240]{2,1,0:T(1,128)S(1)}, u32[]{:S(2)}, u32[]{:S(2)}) async-start(f32[64,1,2240]{2,1,0:T(1,128)} %reshape.1379), calls=%async_computation | async-start | bytes 1179648 | tf_op jit(solution)/shard_map/all_to_all | solution.py:21
  630.0 3.0 copy-start.9
  630.1 3.0 copy-start.11
Sparse Core Ops, SparseCore 0:
  31.3 205.0 all-reduce.2
